TPU v7x, 256 devices: a whole 4x4x8 slice. The times are simulated.
256 devices in a mesh: ctx: 32 (over z, x_hi, core), ch: 8 (over y, x_lo).
Axes of the slice: x: 4 (x_hi: 2, x_lo: 2; x = x_hi * 2 + x_lo), y: 4, z: 8, core: 2. Of those that a mesh axis runs over, the one named last changes fastest.
Arguments:
- values: bfloat16 [2, 131072, 1024], P(None, 'ctx', 'ch'), may hold values from -6 to 6
- gate: bfloat16 [2, 131072, 1024], P(None, 'ctx', 'ch'), may hold values from -6 to 6
- cotangent: bfloat16 [2, 131072, 1024], P(None, 'ctx', 'ch'), may hold values from -1.1953125 to 1.1953125
- factor_one: bfloat16 [256, 512, 512], P('ctx', 'ch'), may hold values from -0.25 to 0.25
- factor_two: bfloat16 [512, 256, 256], P('ctx', 'ch'), may hold values from -0.375 to 0.375
Outputs:
- d_values: bfloat16 [2, 131072, 1024], P(None, 'ctx', 'ch')
- d_gate: bfloat16 [2, 131072, 1024], P(None, 'ctx', 'ch')
- grad_one: float32 [256, 512, 512], P('ctx', 'ch')
- grad_two: float32 [512, 256, 256], P('ctx', 'ch')
All inputs are finite; a program needn't handle non-finite values.
Results may differ from a plain program's by a relative error of at most 0.015.
Values may be sent and summed in bfloat16 or wider, within the bound.
A program may use at most 64 MiB of HBM per device.

v0:
```python
import jax
import jax.numpy as jnp
from jax import lax
from jax.sharding import PartitionSpec as P


def per_device(values, gate, cotangent, factor_one, factor_two):
    seq_count, token_rows, chan_count = values.shape
    blocks_first = factor_one.shape[0]
    order_first = factor_one.shape[2]
    blocks_second = factor_two.shape[0]
    order_second = factor_two.shape[2]
    gated = (values.astype(jnp.float32) * gate.astype(jnp.float32)).astype(jnp.bfloat16)
    inputs = gated.reshape(seq_count, blocks_first, order_first, chan_count)
    whole_first = lax.all_gather(factor_one, "ch", axis=1, tiled=True)
    mixed = jnp.einsum(
        "ikj,sijc->sikc", whole_first, inputs, preferred_element_type=jnp.float32
    ).astype(jnp.bfloat16)
    moved = lax.all_to_all(mixed, "ctx", split_axis=2, concat_axis=1, tiled=True)
    upstream = cotangent.reshape(seq_count, blocks_second, order_second, chan_count)
    back_two = jnp.einsum(
        "kmi,skmc->sikc",
        lax.all_gather(factor_two, "ch", axis=1, tiled=True),
        upstream,
        preferred_element_type=jnp.float32,
    ).astype(jnp.bfloat16)
    term_two = jnp.einsum("skmc,sikc->kmi", upstream, moved, preferred_element_type=jnp.float32)
    returned = lax.all_to_all(back_two, "ctx", split_axis=1, concat_axis=2, tiled=True)
    grad_input = jnp.einsum(
        "ikj,sikc->sijc", whole_first, returned, preferred_element_type=jnp.float32
    )
    term_one = jnp.einsum("sikc,sijc->ikj", returned, inputs, preferred_element_type=jnp.float32)
    grad_one, grad_two = (
        lax.psum_scatter(
            term_one.astype(jnp.bfloat16), "ch", scatter_dimension=1, tiled=True
        ).astype(jnp.float32),
        lax.psum_scatter(
            term_two.astype(jnp.bfloat16), "ch", scatter_dimension=1, tiled=True
        ).astype(jnp.float32),
    )
    grad_input = grad_input.reshape(seq_count, token_rows, chan_count)
    d_values = (grad_input * gate.astype(jnp.float32)).astype(jnp.bfloat16)
    d_gate = (grad_input * values.astype(jnp.float32)).astype(jnp.bfloat16)
    return (d_values, d_gate, grad_one, grad_two)


def solution(mesh):
    in_specs = (
        P(None, "ctx", "ch"),
        P(None, "ctx", "ch"),
        P(None, "ctx", "ch"),
        P("ctx", "ch", None),
        P("ctx", "ch", None),
    )
    out_specs = (
        P(None, "ctx", "ch"),
        P(None, "ctx", "ch"),
        P("ctx", "ch", None),
        P("ctx", "ch", None),
    )
    return jax.shard_map(
        per_device, mesh=mesh, in_specs=in_specs, out_specs=out_specs, check_vma=False
    )
```

profile of v0, /device:TPU:42, one launch (start us, length us, event | category | flops | bytes accessed | tf_op | source)
XLA Modules:
  0.0 435.4 jit_solution(7930363892552423465)
XLA Ops:
  7.2 0.0 all-gather.3.cloned.1.call-start
  7.2 0.7 all-gather.3.cloned.1.call-update
  7.9 0.0 all-gather.5.cloned.1.call-start
  7.9 0.7 all-gather.5.cloned.1.call-update
  8.6 0.0 reduce-scatter.5.cloned.1.call-start
  8.7 56.6 %all-gather.3.cloned.1.call-done = bf16[16,256,256]{2,1,0:T(8,128)(2,1)} async-done(((bf16[16,32,256]{2,1,0:T(8,128)(2,1)}), bf16[16,256,256]{2,1,0:T(8,128)(2,1)}) %all-gather.3.cloned.1.call-update) | async-done | bytes 2097168 | tf_op jit(solution)/shard_map/all_gather | solution.py:23
  65.3 3.0 convert_bitcast_fusion.1
  68.3 3.9 copy.30
  72.2 60.0 %all_to_all.36 = bf16[2,256,16,128]{3,0,2,1:T(2,128)(2,1)S(1)} all-to-all(bf16[2,256,16,128]{3,0,2,1:T(2,128)(2,1)} %copy.30), channel_id=1, replica_groups=mesh['ctx'=32,'ch'=8] {'ctx'}, dimensions={1} | all-to-all | bytes 4194304 | tf_op jit(solution)/shard_map/all_to_all | solution.py:28
  132.2 0.3 copy.31
  132.4 0.5 copy.32
  132.9 49.9 %all-gather.5.cloned.1.call-done = bf16[8,512,512]{2,1,0:T(8,128)(2,1)} async-done(((bf16[8,64,512]{2,1,0:T(8,128)(2,1)}), bf16[8,512,512]{2,1,0:T(8,128)(2,1)}) %all-gather.5.cloned.1.call-update) | async-done | bytes 4194320 | tf_op jit(solution)/shard_map/all_gather | solution.py:15
  182.8 5.5 %fusion.7 = f32[2,8,512,128]{2,3,0,1:T(8,128)} fusion(bf16[8,512,512]{2,1,0:T(8,128)(2,1)} %all-gather.5.cloned.1.call-done, bf16[2,8,512,128]{3,2,1,0:T(8,128)(2,1)S(1)} %bitcast.52), kind=kOutput, calls=%fused_computation.12 | convolution fusion | flops 1073741824 | bytes 10485760 | tf_op jit(solution)/shard_map/ikj,sikc->sijc/dot_general | solution.py:29
  188.3 5.3 %copy.34 = f32[2,8,512,128]{3,2,1,0:T(8,128)} copy(f32[2,8,512,128]{2,3,0,1:T(8,128)} %fusion.7) | data formatting | bytes 8388608 | tf_op jit(solution)/shard_map/ikj,sikc->sijc/transpose | solution.py:29
  193.6 0.0 copy-start.1
  193.6 6.7 %fusion.1 = (bf16[2,4096,128]{2,1,0:T(8,128)(2,1)}, bf16[2,4096,128]{2,1,0:T(8,128)(2,1)}, bf16[2,4096,128]{2,1,0:T(8,128)(2,1)S(1)}) fusion(bf16[2,4096,128]{2,1,0:T(8,128)(2,1)} %param.5, f32[2,8,512,128]{3,2,1,0:T(8,128)} %copy.34, bf16[2,4096,128]{2,1,0:T(8,128)(2,1)} %param.6), kind=kLoop, calls=%fused_computation.5 | loop fusion | flops 8388608 | bytes 14680064 | tf_op jit(solution)/shard_map/convert_element_type | solution.py:43
  200.3 0.0 copy-start
  200.3 1.3 copy-done
  201.7 0.0 copy-done.1
  201.7 2.8 convert_bitcast_fusion
  204.4 6.2 %copy.36 = bf16[2,8,512,128]{3,0,1,2:T(2,128)(2,1)} copy(bf16[2,8,512,128]{2,3,0,1:T(8,128)(2,1)} %convert_bitcast_fusion) | data formatting | bytes 4194304 | tf_op jit(solution)/shard_map/convert_element_type | solution.py:18
  210.7 60.0 %all_to_all.37 = bf16[2,8,512,128]{3,0,1,2:T(2,128)(2,1)S(1)} all-to-all(bf16[2,8,512,128]{3,0,1,2:T(2,128)(2,1)} %copy.36), channel_id=1, replica_groups=mesh['ctx'=32,'ch'=8] {'ctx'}, dimensions={2} | all-to-all | bytes 4194304 | tf_op jit(solution)/shard_map/all_to_all | solution.py:19
  270.6 0.0 copy-start.2
  270.6 0.5 copy.37
  271.2 1.0 copy-done.2
  272.2 2.8 fusion.24
  275.0 4.6 %copy.40 = bf16[16,256,256]{2,0,1:T(8,128)(2,1)} copy(bf16[16,256,256]{1,2,0:T(8,128)(2,1)} %fusion.24) | data formatting | bytes 4194304 | tf_op jit(solution)/shard_map/convert_element_type | solution.py:38
  279.6 0.0 reduce-scatter.5.cloned.1.call-update
  279.6 0.0 reduce-scatter.3.cloned.1.call-start
  279.7 4.8 %bitcast_convert_fusion = bf16[8,512,512]{2,1,0:T(8,128)(2,1)} fusion(bf16[2,8,512,128]{3,2,1,0:T(8,128)(2,1)S(1)} %bitcast.53, bf16[2,8,512,128]{3,2,1,0:T(8,128)(2,1)} %bitcast.55), kind=kOutput, calls=%fused_computation | convolution fusion | flops 1075838976 | bytes 8388608 | tf_op jit(solution)/shard_map/sikc,sijc->ikj/dot_general | solution.py:32
  284.5 0.0 reduce-scatter.3.cloned.1.call-update
  284.5 46.0 %reduce-scatter.5.cloned.1.call-done = bf16[16,32,256]{2,0,1:T(8,128)(2,1)} async-done(((bf16[16,256,256]{2,0,1:T(8,128)(2,1)}), bf16[16,32,256]{2,0,1:T(8,128)(2,1)}) %reduce-scatter.5.cloned.1.call-update) | async-done | bytes 262160 | tf_op jit(solution)/shard_map/reduce_scatter | solution.py:37
  330.5 1.8 copy.41
  332.3 94.4 %reduce-scatter.3.cloned.1.call-done = bf16[8,64,512]{2,1,0:T(8,128)(2,1)} async-done(((bf16[8,512,512]{2,1,0:T(8,128)(2,1)}), bf16[8,64,512]{2,1,0:T(8,128)(2,1)}) %reduce-scatter.3.cloned.1.call-update) | async-done | bytes 524304 | tf_op jit(solution)/shard_map/reduce_scatter | solution.py:34
  426.7 2.1 convert_element_type.52
Async XLA Ops:
  7.2 58.1 %all-gather.3.cloned.1.call-start = ((), (), s32[]{:S(2)}) async-start(), calls=%async_computation.4 | async-start | bytes 2359296 | tf_op jit(solution)/shard_map/all_gather | solution.py:23
  7.9 174.9 %all-gather.5.cloned.1.call-start = ((), (), s32[]{:S(2)}) async-start(), calls=%async_computation.5 | async-start | bytes 4718592 | tf_op jit(solution)/shard_map/all_gather | solution.py:15
  8.6 321.9 %reduce-scatter.5.cloned.1.call-start = ((), (), s32[]{:S(2)}) async-start(), calls=%async_computation.7 | async-start | bytes 2359296 | tf_op jit(solution)/shard_map/reduce_scatter | solution.py:37
  193.6 8.0 %copy-start.1 = (bf16[8,512,512]{2,1,0:T(8,128)(2,1)S(1)}, bf16[8,512,512]{2,1,0:T(8,128)(2,1)}, u32[]{:S(2)}) copy-start(bf16[8,512,512]{2,1,0:T(8,128)(2,1)} %all-gather.5.cloned.1.call-done) | copy-start | bytes 12582916
  200.3 1.3 copy-start
  270.6 1.6 copy-start.2
  279.6 147.1 %reduce-scatter.3.cloned.1.call-start = ((), (), s32[]{:S(2)}) async-start(), calls=%async_computation.6 | async-start | bytes 4718592 | tf_op jit(solution)/shard_map/reduce_scatter | solution.py:34
Sparse Core Ops, SparseCore 0:
  9.8 55.4 all-gather.2
  67.1 115.7 all-gather.4
  279.7 50.7 reduce-scatter.4
  332.9 93.7 reduce-scatter.2
where the time goes:
time: 438 us; the launch traced here: 435 us
  waiting for transfers between devices  248 us (57%)
  blocking collectives  120 us (27%)
  local copies, waits for them, and re-layouts  25.6 us (6%)
  matrix products  18.8 us (4%)
  between operations  13.8 us (3%)
  other arithmetic  8.84 us (2%)
    reduce_scatter x1, waiting for transfers between devices, per_device(): lax.psum_scatter(term_one.astype(jnp.bfloat16), 'ch', scatter_dimension=1...  94.4 us
    all_to_all x1, blocking collectives, per_device(): lax.all_to_all(mixed, 'ctx', split_axis=2, concat_axis=1, tiled=True)  60 us
    all_to_all x1, blocking collectives, per_device(): lax.all_to_all(back_two, 'ctx', split_axis=1, concat_axis=2, tiled=True)  60 us
    all_gather x1, waiting for transfers between devices, per_device(): lax.all_gather(factor_two, 'ch', axis=1, tiled=True)  56.6 us
    all_gather x1, waiting for transfers between devices, per_device(): whole_first = lax.all_gather(factor_one, 'ch', axis=1, tiled=True)  49.9 us
    reduce_scatter x1, waiting for transfers between devices, per_device(): lax.psum_scatter(term_two.astype(jnp.bfloat16), 'ch', scatter_dimension=1...  46 us
  transfers between devices with their start and end apart: 4, of which 4 were waited for; matrix products, arithmetic and copies ran while one was open for 3% of the time, Pallas kernels for 0%

commit v1 on v0

v1 whole, which is shorter than its diff:
```python
import jax
import jax.numpy as jnp
from jax import lax
from jax.experimental import pallas as pl
from jax.experimental.pallas import tpu as pltpu
from jax.sharding import PartitionSpec as P

MESH = pl.DeviceIdType.MESH
F32, BF16 = jnp.float32, jnp.bfloat16
N_CTX, N_CH = 32, 8
PAIRS = N_CTX // 2


def dot(a, b, dims):
    return lax.dot_general(a, b, (dims, ((), ())), preferred_element_type=F32)


class Place:
    def __init__(self):
        self.a = lax.axis_index("ctx")
        self.h = lax.axis_index("ch")
        self.y, self.xl = self.h // 2, self.h % 2
        self.xp = (self.a, self.piece(0, 1))
        self.yp = (self.a, self.piece(1, 0))
        self.ym = (self.a, self.piece(3, 0))

    def piece(self, dy, dx):
        xl = 1 - self.xl if dx else self.xl
        return lax.rem(self.y + dy, 4) * 2 + xl


def remote(src, dst, ssem, rsem, dev):
    return pltpu.make_async_remote_copy(
        src_ref=src, dst_ref=dst, send_sem=ssem, recv_sem=rsem, device_id=dev, device_id_type=MESH
    )


class Gather:
    def __init__(self, at, buf, ssem, rsem):
        self.at, self.buf, self.ssem, self.rsem = at, buf, ssem, rsem
        p = at.piece
        self.plan = (
            (p(0, 0), at.xp, p(0, 1)),
            (p(0, 0), at.yp, p(3, 0)),
            (p(0, 0), at.ym, p(1, 0)),
            (p(0, 1), at.yp, p(3, 1)),
            (p(0, 1), at.ym, p(1, 1)),
            (p(3, 0), at.yp, p(2, 0)),
            (p(1, 1), at.ym, p(2, 1)),
        )

    def copy(self, k, arrives=False):
        sent, dev, came = self.plan[k]
        ref = self.buf.at[came if arrives else sent]
        return remote(ref, ref, self.ssem.at[k], self.rsem.at[k], dev)

    def send(self, *ks):
        for k in ks:
            self.copy(k).start()

    def wait(self, *ks):
        for k in ks:
            self.copy(k, True).wait_recv()

    def drain(self):
        for k in range(7):
            self.copy(k).wait_send()


class Scatter:
    def __init__(self, at, part, got, ssem, rsem):
        self.at, self.part, self.got, self.ssem, self.rsem = at, part, got, ssem, rsem
        p = at.piece
        self.plan = (
            (p(2, 0), at.yp),
            (p(2, 1), at.ym),
            (p(1, 0), at.yp),
            (p(1, 1), at.yp),
            (p(3, 1), at.ym),
            (p(3, 0), at.ym),
            (p(0, 1), at.xp),
        )

    def copy(self, k):
        sent, dev = self.plan[k]
        return remote(self.part.at[sent], self.got.at[k], self.ssem.at[k], self.rsem.at[k], dev)

    def send(self, *ks):
        for k in ks:
            self.copy(k).start()

    def wait(self, *ks):
        for k in ks:
            self.copy(k).wait_recv()

    def add(self, piece, *ks):
        n = self.part.shape[1]

        def body(i, _):
            total = self.part[piece, i].astype(F32)
            for k in ks:
                total += self.got[k, i].astype(F32)
            self.part[piece, i] = total.astype(BF16)
            return 0

        lax.fori_loop(0, n, body, 0)

    def first(self):
        self.send(0, 1, 3, 5)

    def second(self):
        self.wait(0)
        self.add(self.at.piece(1, 0), 0)
        self.send(2)
        self.wait(1)
        self.add(self.at.piece(3, 1), 1)
        self.send(4)

    def third(self):
        self.wait(3, 4)
        self.add(self.at.piece(0, 1), 3, 4)
        self.send(6)

    def last(self, out):
        self.wait(2, 5, 6)
        mine = self.at.piece(0, 0)

        def body(i, _):
            total = self.part[mine, i].astype(F32)
            for k in (2, 5, 6):
                total += self.got[k, i].astype(F32)
            out[i] = total
            return 0

        lax.fori_loop(0, self.part.shape[1], body, 0)

    def drain(self):
        for k in range(7):
            self.copy(k).wait_send()


def kernel(
    v_hbm, g_hbm, c_hbm, f1_hbm, f2_hbm,
    dv_hbm, dg_hbm, o1_hbm, o2_hbm,
    val, gate, up, f1, f2, gated, back, sendb, ret, mix, mov, movt, part1, got1, part2, got2, out1, out2,
    lsem, osem, g2s, g2r, g1s, g1r, s1s, s1r, s2s, s2r, bs, br, ms, mr,
):
    at = Place()
    a, h = at.a, at.h
    pair0 = a // 2
    core = a % 2

    loads = []

    def load(src, dst):
        cp = pltpu.make_async_copy(src, dst, lsem.at[len(loads)])
        cp.start()
        loads.append(cp)
        return cp

    f2_in = load(f2_hbm, f2.at[h])
    f1_in = load(f1_hbm, f1.at[h])
    rest = []
    for s in range(2):
        lanes = pl.ds(128 * s, 128)
        rest.append(load(c_hbm.at[s], up.at[:, lanes]))
        rest.append(load(v_hbm.at[s], val.at[:, lanes]))
        rest.append(load(g_hbm.at[s], gate.at[:, lanes]))

    barrier = pltpu.get_barrier_semaphore()

    def greet(k, _):
        pl.semaphore_signal(barrier, inc=1, device_id=(lax.rem(a + k, N_CTX), h), device_id_type=MESH)
        return 0

    for dev in (at.xp, at.yp, at.ym):
        pl.semaphore_signal(barrier, inc=1, device_id=dev, device_id_type=MESH)
    lax.fori_loop(1, N_CTX, greet, 0)
    pl.semaphore_wait(barrier, N_CTX - 1 + 3)

    two = Gather(at, f2, g2s, g2r)
    one = Gather(at, f1, g1s, g1r)
    f2_in.wait()
    two.send(0, 1, 2)

    for cp in rest:
        cp.wait()

    def multiply(k, _):
        rows = pl.ds(pl.multiple_of(k * 512, 512), 512)
        gated[k] = (val[rows, :].astype(F32) * gate[rows, :].astype(F32)).astype(BF16)
        return 0

    lax.fori_loop(0, 8, multiply, 0)

    two.wait(0)
    two.send(3, 4)
    two.wait(1)
    two.send(5)
    two.wait(4)
    two.send(6)
    f1_in.wait()
    one.send(0, 1, 2)
    two.wait(2, 3, 5, 6)

    def back_block(k, _):
        w = f2[:, k].reshape(256, 256)
        u = up[pl.ds(pl.multiple_of(k * 256, 256), 256), :]
        back[k] = dot(w, u, ((0,), (0,))).astype(BF16)
        return 0

    lax.fori_loop(0, 16, back_block, 0)

    r = lax.broadcasted_iota(jnp.int32, (256, 256), 0)
    c = lax.broadcasted_iota(jnp.int32, (256, 256), 1)
    swap = jnp.where(((r >> 4) == (c & 15)) & ((r & 15) == (c >> 4)), 1.0, 0.0).astype(BF16)

    def back_copy(dst, slot):
        return remote(
            sendb.at[dst], ret.at[:, pl.ds(pl.multiple_of(16 * slot, 16), 16), :], bs.at[dst], br.at[slot], (dst, h)
        )

    def back_send(k, _):
        p = lax.rem(pair0 + k, PAIRS)
        x = back[:, pl.ds(pl.multiple_of(16 * p, 16), 16), :].reshape(256, 256)
        t = dot(swap, x, ((1,), (0,))).astype(BF16).reshape(2, 8, 16, 256)
        sendb[2 * p] = t[0]
        sendb[2 * p + 1] = t[1]

        @pl.when(k > 0)
        def _():
            back_copy(2 * p + core, a).start()

        back_copy(2 * p + 1 - core, a).start()
        return 0

    lax.fori_loop(0, PAIRS, back_send, 0)
    ret[:, pl.ds(pl.multiple_of(16 * a, 16), 16), :] = sendb[a]

    one.wait(0)
    one.send(3, 4)
    one.wait(1)
    one.send(5)
    one.wait(4)
    one.send(6)
    one.wait(2, 3, 5, 6)

    def mix_block(i, _):
        mix[i] = dot(f1[:, i].reshape(512, 512), gated[i], ((1,), (0,))).astype(BF16)
        return 0

    lax.fori_loop(0, 8, mix_block, 0)

    def mix_copy(dst, slot):
        return remote(
            mix.at[:, pl.ds(pl.multiple_of(16 * dst, 16), 16), :], mov.at[slot], ms.at[dst], mr.at[slot], (dst, h)
        )

    def mix_send(k, _):
        p = lax.rem(pair0 + k, PAIRS)

        @pl.when(k > 0)
        def _():
            mix_copy(2 * p + core, a).start()

        mix_copy(2 * p + 1 - core, a).start()
        return 0

    lax.fori_loop(0, PAIRS, mix_send, 0)
    mov[a] = mix[:, pl.ds(pl.multiple_of(16 * a, 16), 16), :]

    def back_wait(k, _):
        src = lax.rem(a + k, N_CTX)
        back_copy(src, src).wait_recv()
        return 0

    lax.fori_loop(1, N_CTX, back_wait, 0)

    def first_block(i, _):
        part1[:, i] = dot(ret[i], gated[i], ((1,), (1,))).astype(BF16).reshape(8, 64, 512)
        grad = dot(f1[:, i].reshape(512, 512), ret[i], ((0,), (0,)))
        rows = pl.ds(pl.multiple_of(i * 512, 512), 512)
        v, g = val[rows, :].astype(F32), gate[rows, :].astype(F32)
        val[rows, :] = (grad * g).astype(BF16)
        gate[rows, :] = (grad * v).astype(BF16)
        return 0

    lax.fori_loop(0, 8, first_block, 0)

    rs1 = Scatter(at, part1, got1, s1s, s1r)
    rs2 = Scatter(at, part2, got2, s2s, s2r)
    rs1.first()
    stores = []

    def store(src, dst):
        cp = pltpu.make_async_copy(src, dst, osem.at[len(stores)])
        cp.start()
        stores.append(cp)

    for s in range(2):
        lanes = pl.ds(128 * s, 128)
        store(val.at[:, lanes], dv_hbm.at[s])
        store(gate.at[:, lanes], dg_hbm.at[s])

    def mix_take(k, _):
        p = lax.rem(pair0 + PAIRS - k, PAIRS)

        @pl.when(k > 0)
        def _():
            mix_copy(2 * p + core, 2 * p + core).wait_recv()

        mix_copy(2 * p + 1 - core, 2 * p + 1 - core).wait_recv()
        x = mov[pl.ds(2 * p, 2)].reshape(256, 256)
        t = dot(swap, x, ((1,), (0,))).astype(BF16).reshape(16, 16, 256)
        movt[:, pl.ds(pl.multiple_of(16 * p, 16), 16), :] = t
        return 0

    lax.fori_loop(0, 4, mix_take, 0)
    rs1.second()
    lax.fori_loop(4, 8, mix_take, 0)
    rs1.third()
    lax.fori_loop(8, PAIRS, mix_take, 0)

    def second_block(k, _):
        u = up[pl.ds(pl.multiple_of(k * 256, 256), 256), :]
        part2[:, k] = dot(u, movt[k], ((1,), (1,))).astype(BF16).reshape(8, 32, 256)
        return 0

    lax.fori_loop(0, 16, second_block, 0)
    rs2.first()
    rs1.last(out1)
    store(out1, o1_hbm)
    rs2.second()
    rs2.third()
    rs2.last(out2)
    store(out2, o2_hbm)

    def drain(k, _):
        dst = lax.rem(a + k, N_CTX)
        back_copy(dst, a).wait_send()
        mix_copy(dst, a).wait_send()
        return 0

    lax.fori_loop(1, N_CTX, drain, 0)
    for x in (one, two, rs1, rs2):
        x.drain()
    for cp in stores:
        cp.wait()


def per_device(values, gate, cotangent, factor_one, factor_two):
    vm = pltpu.VMEM
    dma = pltpu.SemaphoreType.DMA
    shapes = (
        jax.ShapeDtypeStruct(values.shape, BF16),
        jax.ShapeDtypeStruct(values.shape, BF16),
        jax.ShapeDtypeStruct(factor_one.shape, F32),
        jax.ShapeDtypeStruct(factor_two.shape, F32),
    )
    scratch = [
        vm((4096, 256), BF16), vm((4096, 256), BF16), vm((4096, 256), BF16),
        vm((8, 8, 64, 512), BF16), vm((8, 16, 32, 256), BF16),
        vm((8, 512, 256), BF16),
        vm((16, 256, 256), BF16),
        vm((32, 8, 16, 256), BF16),
        vm((8, 512, 256), BF16),
        vm((8, 512, 256), BF16),
        vm((32, 8, 16, 256), BF16),
        vm((16, 256, 256), BF16),
        vm((8, 8, 64, 512), BF16), vm((7, 8, 64, 512), BF16),
        vm((8, 16, 32, 256), BF16), vm((7, 16, 32, 256), BF16),
        vm((8, 64, 512), F32), vm((16, 32, 256), F32),
        dma((8,)), dma((6,)),
        dma((7,)), dma((7,)), dma((7,)), dma((7,)), dma((7,)), dma((7,)), dma((7,)), dma((7,)),
        dma((32,)), dma((32,)), dma((32,)), dma((32,)),
    ]
    anywhere = pl.BlockSpec(memory_space=pl.ANY)
    return pl.pallas_call(
        kernel,
        out_shape=shapes,
        in_specs=[anywhere] * 5,
        out_specs=(anywhere,) * 4,
        scratch_shapes=scratch,
        compiler_params=pltpu.CompilerParams(
            collective_id=0, has_side_effects=True, vmem_limit_bytes=56 * 1024 * 1024
        ),
        name="monarch_backward",
    )(values, gate, cotangent, factor_one, factor_two)


def solution(mesh):
    tokens = P(None, "ctx", "ch")
    rows = P("ctx", "ch", None)
    return jax.shard_map(
        per_device,
        mesh=mesh,
        in_specs=(tokens, tokens, tokens, rows, rows),
        out_specs=(tokens, tokens, rows, rows),
        check_vma=False,
    )
```

time: 438 us -> 173 us (0.39)
  the two profiles are of different devices: /device:TPU:42 before, /device:TPU:37 now
where the time goes in v1:
time: 173 us
  Pallas kernels  165 us (95%)
  local copies, waits for them, and re-layouts  7.34 us (4%)
    pallas_call x1, Pallas kernels, per_device(): pl.pallas_call(kernel, out_shape=shapes, in_specs=[anywhere] * 5, out_spe...  165 us
    unnamed x10, local copies, waits for them, and re-layouts  7.34 us

profile of v1, /device:TPU:37, one launch (start us, length us, event | category | flops | bytes accessed | tf_op | source)
XLA Modules:
  0.0 172.6 jit_solution(4400750625630465903)
XLA Ops:
  0.6 164.6 %monarch_backward.1 = (bf16[2,4096,128]{2,1,0:T(8,128)(2,1)}, bf16[2,4096,128]{2,1,0:T(8,128)(2,1)}, f32[8,64,512]{2,1,0:T(8,128)}, f32[16,32,256]{2,1,0:T(8,128)}) custom-call(bf16[2,4096,128]{2,1,0:T(8,128)(2,1)} %v_hbm.1, bf16[2,4096,128]{2,1,0:T(8,128)(2,1)} %g_hbm.1, bf16[2,4096,128]{2,1,0:T(8,128)(2,1)} %c_hbm.1, bf16[8,64,512]{2,1,0:T(8,128)(2,1)} %f1_hbm.1, ...), custom_call_target="tpu_custom_call" | custom-call | tf_op jit(solution)/shard_map/monarch_backward/pallas_call | solution.py:378
  165.2 0.0 copy-start
  165.2 3.2 %copy.13 = bf16[2,4096,128]{2,1,0:T(8,128)(2,1)} copy(bf16[2,4096,128]{2,1,0:T(8,128)(2,1)} %get-tuple-element.8) | data formatting | bytes 4194304
  168.4 0.0 copy-done
  168.4 0.0 copy-start.1
  168.4 1.3 copy.14
  169.8 0.6 copy-done.1
  170.4 0.0 copy-start.2
  170.4 1.0 copy.15
  171.4 0.4 copy-done.2
  171.8 0.8 copy.16
Async XLA Ops:
  165.2 3.2 %copy-start = (bf16[2,4096,128]{2,1,0:T(8,128)(2,1)S(1)}, bf16[2,4096,128]{2,1,0:T(8,128)(2,1)}, u32[]{:S(2)}) copy-start(bf16[2,4096,128]{2,1,0:T(8,128)(2,1)} %get-tuple-element.9) | copy-start | bytes 6291460
  168.4 2.0 %copy-start.1 = (f32[8,64,512]{2,1,0:T(8,128)S(1)}, f32[8,64,512]{2,1,0:T(8,128)}, u32[]{:S(2)}) copy-start(f32[8,64,512]{2,1,0:T(8,128)} %get-tuple-element.10) | copy-start | bytes 3145732
  170.4 1.4 copy-start.2

commit v2 on v1

--- a/solution.py
+++ b/solution.py
@@ -142,13 +142,14 @@
 def kernel(
     v_hbm, g_hbm, c_hbm, f1_hbm, f2_hbm,
     dv_hbm, dg_hbm, o1_hbm, o2_hbm,
-    val, gate, up, f1, f2, gated, back, sendb, ret, mix, mov, movt, part1, got1, part2, got2, out1, out2,
-    lsem, osem, g2s, g2r, g1s, g1r, s1s, s1r, s2s, s2r, bs, br, ms, mr,
+    val, gate, up, f1, f2_own, f2_far, f2_near, gated, back, sendb, ret, mix, mov, movt,
+    part1, got1, part2f, got2f, part2n, got2n, out1, out2f, out2n, out2,
+    lsem, osem, g2fs, g2fr, g2ns, g2nr, g1s, g1r, s1s, s1r, s2fs, s2fr, s2ns, s2nr, bs, br, ms, mr,
 ):
     at = Place()
     a, h = at.a, at.h
+    z, xh, core = a // 4, (a // 2) % 2, a % 2
     pair0 = a // 2
-    core = a % 2
 
     loads = []
 
@@ -158,7 +159,7 @@
         loads.append(cp)
         return cp
 
-    f2_in = load(f2_hbm, f2.at[h])
+    f2_in = load(f2_hbm, f2_own)
     f1_in = load(f1_hbm, f1.at[h])
     rest = []
     for s in range(2):
@@ -178,10 +179,21 @@
     lax.fori_loop(1, N_CTX, greet, 0)
     pl.semaphore_wait(barrier, N_CTX - 1 + 3)
 
-    two = Gather(at, f2, g2s, g2r)
+    far = Gather(at, f2_far, g2fs, g2fr)
+    near = Gather(at, f2_near, g2ns, g2nr)
     one = Gather(at, f1, g1s, g1r)
+
     f2_in.wait()
-    two.send(0, 1, 2)
+    turn = lax.rem(256 - 32 * lax.rem(z + 3, 8), 256)
+
+    def turn_block(k, _):
+        x = pltpu.roll(f2_own[k].astype(F32), turn, 1).astype(BF16)
+        f2_far[h, k] = x[:, :128]
+        f2_near[h, k] = x[:, 128:]
+        return 0
+
+    lax.fori_loop(0, 16, turn_block, 0)
+    far.send(0, 1, 2)
 
     for cp in rest:
         cp.wait()
@@ -193,23 +205,14 @@
 
     lax.fori_loop(0, 8, multiply, 0)
 
-    two.wait(0)
-    two.send(3, 4)
-    two.wait(1)
-    two.send(5)
-    two.wait(4)
-    two.send(6)
-    f1_in.wait()
-    one.send(0, 1, 2)
-    two.wait(2, 3, 5, 6)
-
-    def back_block(k, _):
-        w = f2[:, k].reshape(256, 256)
-        u = up[pl.ds(pl.multiple_of(k * 256, 256), 256), :]
-        back[k] = dot(w, u, ((0,), (0,))).astype(BF16)
-        return 0
-
-    lax.fori_loop(0, 16, back_block, 0)
+    far.wait(0)
+    far.send(3, 4)
+    far.wait(1)
+    far.send(5)
+    far.wait(4)
+    far.send(6)
+    near.send(0, 1, 2)
+    far.wait(2, 3, 5, 6)
 
     r = lax.broadcasted_iota(jnp.int32, (256, 256), 0)
     c = lax.broadcasted_iota(jnp.int32, (256, 256), 1)
@@ -220,21 +223,44 @@
             sendb.at[dst], ret.at[:, pl.ds(pl.multiple_of(16 * slot, 16), 16), :], bs.at[dst], br.at[slot], (dst, h)
         )
 
-    def back_send(k, _):
-        p = lax.rem(pair0 + k, PAIRS)
-        x = back[:, pl.ds(pl.multiple_of(16 * p, 16), 16), :].reshape(256, 256)
-        t = dot(swap, x, ((1,), (0,))).astype(BF16).reshape(2, 8, 16, 256)
-        sendb[2 * p] = t[0]
-        sendb[2 * p + 1] = t[1]
-
-        @pl.when(k > 0)
-        def _():
-            back_copy(2 * p + core, a).start()
-
-        back_copy(2 * p + 1 - core, a).start()
-        return 0
-
-    lax.fori_loop(0, PAIRS, back_send, 0)
+    def back_half(w_ref, first):
+        def block(k, _):
+            w = w_ref[:, k].reshape(256, 128)
+            u = up[pl.ds(pl.multiple_of(k * 256, 256), 256), :]
+            back[k] = dot(w, u, ((0,), (0,))).astype(BF16)
+            return 0
+
+        lax.fori_loop(0, 16, block, 0)
+
+        def send(k, _):
+            xt = lax.rem(xh + k, 2)
+            p = lax.rem(z + first + k // 2, 8) * 2 + xt
+            row = pl.multiple_of((k // 2) * 32 + xt * 16, 16)
+            x = back[:, pl.ds(row, 16), :].reshape(256, 256)
+            t = dot(swap, x, ((1,), (0,))).astype(BF16).reshape(2, 8, 16, 256)
+            sendb[2 * p] = t[0]
+            sendb[2 * p + 1] = t[1]
+
+            @pl.when(p != pair0)
+            def _():
+                back_copy(2 * p + core, a).start()
+
+            back_copy(2 * p + 1 - core, a).start()
+            return 0
+
+        lax.fori_loop(0, 8, send, 0)
+
+    back_half(f2_far, 3)
+    near.wait(0)
+    near.send(3, 4)
+    near.wait(1)
+    near.send(5)
+    near.wait(4)
+    near.send(6)
+    f1_in.wait()
+    one.send(0, 1, 2)
+    near.wait(2, 3, 5, 6)
+    back_half(f2_near, 7)
     ret[:, pl.ds(pl.multiple_of(16 * a, 16), 16), :] = sendb[a]
 
     one.wait(0)
@@ -257,9 +283,9 @@
         )
 
     def mix_send(k, _):
-        p = lax.rem(pair0 + k, PAIRS)
-
-        @pl.when(k > 0)
+        p = lax.rem(z + 3 + k // 2, 8) * 2 + lax.rem(xh + k, 2)
+
+        @pl.when(p != pair0)
         def _():
             mix_copy(2 * p + core, a).start()
 
@@ -276,8 +302,17 @@
 
     lax.fori_loop(1, N_CTX, back_wait, 0)
 
-    def first_block(i, _):
+    def grad_one_block(i, _):
         part1[:, i] = dot(ret[i], gated[i], ((1,), (1,))).astype(BF16).reshape(8, 64, 512)
+        return 0
+
+    lax.fori_loop(0, 8, grad_one_block, 0)
+    rs1 = Scatter(at, part1, got1, s1s, s1r)
+    rs2f = Scatter(at, part2f, got2f, s2fs, s2fr)
+    rs2n = Scatter(at, part2n, got2n, s2ns, s2nr)
+    rs1.first()
+
+    def grad_input_block(i, _):
         grad = dot(f1[:, i].reshape(512, 512), ret[i], ((0,), (0,)))
         rows = pl.ds(pl.multiple_of(i * 512, 512), 512)
         v, g = val[rows, :].astype(F32), gate[rows, :].astype(F32)
@@ -285,11 +320,7 @@
         gate[rows, :] = (grad * v).astype(BF16)
         return 0
 
-    lax.fori_loop(0, 8, first_block, 0)
-
-    rs1 = Scatter(at, part1, got1, s1s, s1r)
-    rs2 = Scatter(at, part2, got2, s2s, s2r)
-    rs1.first()
+    lax.fori_loop(0, 8, grad_input_block, 0)
     stores = []
 
     def store(src, dst):
@@ -302,37 +333,53 @@
         store(val.at[:, lanes], dv_hbm.at[s])
         store(gate.at[:, lanes], dg_hbm.at[s])
 
-    def mix_take(k, _):
-        p = lax.rem(pair0 + PAIRS - k, PAIRS)
-
-        @pl.when(k > 0)
-        def _():
-            mix_copy(2 * p + core, 2 * p + core).wait_recv()
-
-        mix_copy(2 * p + 1 - core, 2 * p + 1 - core).wait_recv()
-        x = mov[pl.ds(2 * p, 2)].reshape(256, 256)
-        t = dot(swap, x, ((1,), (0,))).astype(BF16).reshape(16, 16, 256)
-        movt[:, pl.ds(pl.multiple_of(16 * p, 16), 16), :] = t
-        return 0
-
-    lax.fori_loop(0, 4, mix_take, 0)
+    def second_half(part, last):
+        def take(k, _):
+            zo = last + 8 - k // 2
+            xt = lax.rem(xh + k, 2)
+            p = lax.rem(z + zo, 8) * 2 + xt
+
+            @pl.when(p != pair0)
+            def _():
+                mix_copy(2 * p + core, 2 * p + core).wait_recv()
+
+            mix_copy(2 * p + 1 - core, 2 * p + 1 - core).wait_recv()
+            x = mov[pl.ds(2 * p, 2)].reshape(256, 256)
+            t = dot(swap, x, ((1,), (0,))).astype(BF16).reshape(16, 16, 256)
+            row = pl.multiple_of((3 - k // 2) * 32 + xt * 16, 16)
+            movt[:, pl.ds(row, 16), :] = t
+            return 0
+
+        lax.fori_loop(0, 8, take, 0)
+
+        def block(k, _):
+            u = up[pl.ds(pl.multiple_of(k * 256, 256), 256), :]
+            part[:, k] = dot(u, movt[k], ((1,), (1,))).astype(BF16).reshape(8, 32, 128)
+            return 0
+
+        lax.fori_loop(0, 16, block, 0)
+
     rs1.second()
-    lax.fori_loop(4, 8, mix_take, 0)
+    second_half(part2f, 5)
+    rs2f.first()
     rs1.third()
-    lax.fori_loop(8, PAIRS, mix_take, 0)
-
-    def second_block(k, _):
-        u = up[pl.ds(pl.multiple_of(k * 256, 256), 256), :]
-        part2[:, k] = dot(u, movt[k], ((1,), (1,))).astype(BF16).reshape(8, 32, 256)
-        return 0
-
-    lax.fori_loop(0, 16, second_block, 0)
-    rs2.first()
+    rs2f.second()
+    second_half(part2n, 9)
+    rs2n.first()
     rs1.last(out1)
     store(out1, o1_hbm)
-    rs2.second()
-    rs2.third()
-    rs2.last(out2)
+    rs2f.third()
+    rs2n.second()
+    rs2f.last(out2f)
+    rs2n.third()
+    rs2n.last(out2n)
+    unturn = 32 * lax.rem(z + 2, 8)
+
+    def unturn_block(k, _):
+        out2[k] = pltpu.roll(jnp.concatenate([out2f[k], out2n[k]], axis=1), unturn, 1)
+        return 0
+
+    lax.fori_loop(0, 16, unturn_block, 0)
     store(out2, o2_hbm)
 
     def drain(k, _):
@@ -342,7 +389,7 @@
         return 0
 
     lax.fori_loop(1, N_CTX, drain, 0)
-    for x in (one, two, rs1, rs2):
+    for x in (far, near, one, rs1, rs2f, rs2n):
         x.drain()
     for cp in stores:
         cp.wait()
@@ -359,19 +406,21 @@
     )
     scratch = [
         vm((4096, 256), BF16), vm((4096, 256), BF16), vm((4096, 256), BF16),
-        vm((8, 8, 64, 512), BF16), vm((8, 16, 32, 256), BF16),
+        vm((8, 8, 64, 512), BF16),
+        vm((16, 32, 256), BF16), vm((8, 16, 32, 128), BF16), vm((8, 16, 32, 128), BF16),
         vm((8, 512, 256), BF16),
-        vm((16, 256, 256), BF16),
+        vm((16, 128, 256), BF16),
         vm((32, 8, 16, 256), BF16),
         vm((8, 512, 256), BF16),
         vm((8, 512, 256), BF16),
         vm((32, 8, 16, 256), BF16),
-        vm((16, 256, 256), BF16),
+        vm((16, 128, 256), BF16),
         vm((8, 8, 64, 512), BF16), vm((7, 8, 64, 512), BF16),
-        vm((8, 16, 32, 256), BF16), vm((7, 16, 32, 256), BF16),
-        vm((8, 64, 512), F32), vm((16, 32, 256), F32),
+        vm((8, 16, 32, 128), BF16), vm((7, 16, 32, 128), BF16),
+        vm((8, 16, 32, 128), BF16), vm((7, 16, 32, 128), BF16),
+        vm((8, 64, 512), F32), vm((16, 32, 128), F32), vm((16, 32, 128), F32), vm((16, 32, 256), F32),
         dma((8,)), dma((6,)),
-        dma((7,)), dma((7,)), dma((7,)), dma((7,)), dma((7,)), dma((7,)), dma((7,)), dma((7,)),
+        *[dma((7,)) for _ in range(12)],
         dma((32,)), dma((32,)), dma((32,)), dma((32,)),
     ]
     anywhere = pl.BlockSpec(memory_space=pl.ANY)

time: 173 us -> 160 us (0.925)
  the two profiles are of different devices: /device:TPU:37 before, /device:TPU:42 now
where the time goes in v2:
time: 160 us; the launch traced here: 159 us
  Pallas kernels  151 us (94%)
  local copies, waits for them, and re-layouts  7.34 us (5%)
    pallas_call x1, Pallas kernels, per_device(): pl.pallas_call(kernel, out_shape=shapes, in_specs=[anywhere] * 5, out_spe...  151 us
    unnamed x10, local copies, waits for them, and re-layouts  7.34 us

profile of v2, /device:TPU:42, one launch (start us, length us, event | category | flops | bytes accessed | tf_op | source)
XLA Modules:
  0.0 159.3 jit_solution(2917210569289619085)
XLA Ops:
  0.6 151.3 %monarch_backward.1 = (bf16[2,4096,128]{2,1,0:T(8,128)(2,1)}, bf16[2,4096,128]{2,1,0:T(8,128)(2,1)}, f32[8,64,512]{2,1,0:T(8,128)}, f32[16,32,256]{2,1,0:T(8,128)}) custom-call(bf16[2,4096,128]{2,1,0:T(8,128)(2,1)} %v_hbm.1, bf16[2,4096,128]{2,1,0:T(8,128)(2,1)} %g_hbm.1, bf16[2,4096,128]{2,1,0:T(8,128)(2,1)} %c_hbm.1, bf16[8,64,512]{2,1,0:T(8,128)(2,1)} %f1_hbm.1, ...), custom_call_target="tpu_custom_call" | custom-call | tf_op jit(solution)/shard_map/monarch_backward/pallas_call | solution.py:427
  152.0 0.0 copy-start
  152.0 3.2 %copy.13 = bf16[2,4096,128]{2,1,0:T(8,128)(2,1)} copy(bf16[2,4096,128]{2,1,0:T(8,128)(2,1)} %get-tuple-element.8) | data formatting | bytes 4194304
  155.2 0.0 copy-done
  155.2 0.0 copy-start.1
  155.2 1.3 copy.14
  156.5 0.6 copy-done.1
  157.1 0.0 copy-start.2
  157.1 1.0 copy.15
  158.1 0.4 copy-done.2
  158.5 0.8 copy.16
Async XLA Ops:
  152.0 3.2 %copy-start = (bf16[2,4096,128]{2,1,0:T(8,128)(2,1)S(1)}, bf16[2,4096,128]{2,1,0:T(8,128)(2,1)}, u32[]{:S(2)}) copy-start(bf16[2,4096,128]{2,1,0:T(8,128)(2,1)} %get-tuple-element.9) | copy-start | bytes 6291460
  155.2 2.0 %copy-start.1 = (f32[8,64,512]{2,1,0:T(8,128)S(1)}, f32[8,64,512]{2,1,0:T(8,128)}, u32[]{:S(2)}) copy-start(f32[8,64,512]{2,1,0:T(8,128)} %get-tuple-element.10) | copy-start | bytes 3145732
  157.1 1.4 copy-start.2

commit v3 on v2

v3 whole, which is shorter than its diff:
```python
import jax
import jax.numpy as jnp
from jax import lax
from jax.experimental import pallas as pl
from jax.experimental.pallas import tpu as pltpu
from jax.sharding import PartitionSpec as P

MESH = pl.DeviceIdType.MESH
F32, BF16 = jnp.float32, jnp.bfloat16
N_CTX, N_CH = 32, 8
PAIRS = N_CTX // 2


def dot(a, b, dims):
    return lax.dot_general(a, b, (dims, ((), ())), preferred_element_type=F32)


class Place:
    def __init__(self):
        self.a = lax.axis_index("ctx")
        self.h = lax.axis_index("ch")
        self.y, self.xl = self.h // 2, self.h % 2
        self.xp = (self.a, self.piece(0, 1))
        self.yp = (self.a, self.piece(1, 0))
        self.ym = (self.a, self.piece(3, 0))

    def piece(self, dy, dx):
        xl = 1 - self.xl if dx else self.xl
        return lax.rem(self.y + dy, 4) * 2 + xl


def remote(src, dst, ssem, rsem, dev):
    return pltpu.make_async_remote_copy(
        src_ref=src, dst_ref=dst, send_sem=ssem, recv_sem=rsem, device_id=dev, device_id_type=MESH
    )


class Gather:
    def __init__(self, at, buf, ssem, rsem, start=0, size=None):
        self.at, self.buf, self.ssem, self.rsem = at, buf, ssem, rsem
        self.blocks = pl.ds(start, buf.shape[1] if size is None else size)
        p = at.piece
        self.plan = (
            (p(0, 0), at.xp, p(0, 1)),
            (p(0, 0), at.yp, p(3, 0)),
            (p(0, 0), at.ym, p(1, 0)),
            (p(0, 1), at.yp, p(3, 1)),
            (p(0, 1), at.ym, p(1, 1)),
            (p(3, 0), at.yp, p(2, 0)),
            (p(1, 1), at.ym, p(2, 1)),
        )

    def copy(self, k, arrives=False):
        sent, dev, came = self.plan[k]
        ref = self.buf.at[came if arrives else sent, self.blocks]
        return remote(ref, ref, self.ssem.at[k], self.rsem.at[k], dev)

    def send(self, *ks):
        for k in ks:
            self.copy(k).start()

    def wait(self, *ks):
        for k in ks:
            self.copy(k, True).wait_recv()

    def relay(self):
        self.wait(0)
        self.send(3, 4)
        self.wait(1)
        self.send(5)
        self.wait(4)
        self.send(6)

    def drain(self):
        for k in range(7):
            self.copy(k).wait_send()


class Direct:
    ORDER = (1, 4, 5, 2, 6, 3, 7)

    def __init__(self, at, part, got, ssem, rsem):
        self.at, self.part, self.got, self.ssem, self.rsem = at, part, got, ssem, rsem

    def copy(self, d):
        there = self.at.piece(d // 2, d % 2)
        if self.got is None:
            mine = self.part.at[self.at.piece(0, 0)]
            return remote(mine, mine, self.ssem.at[d - 1], self.rsem.at[d - 1], (self.at.a, there))
        return remote(self.part.at[there], self.got.at[d - 1], self.ssem.at[d - 1], self.rsem.at[d - 1], (self.at.a, there))

    def send(self):
        for d in self.ORDER:
            self.copy(d).start()

    def wait(self):
        for d in self.ORDER:
            if self.got is None:
                came = self.part.at[self.at.piece((8 - d // 2) % 4, d % 2)]
                remote(came, came, self.ssem.at[d - 1], self.rsem.at[d - 1], self.at.xp).wait_recv()
            else:
                self.copy(d).wait_recv()

    def last(self, out):
        self.wait()
        mine = self.at.piece(0, 0)

        def body(i, _):
            total = self.part[mine, i].astype(F32)
            for k in range(7):
                total += self.got[k, i].astype(F32)
            out[i] = total
            return 0

        lax.fori_loop(0, self.part.shape[1], body, 0)

    def drain(self):
        for d in self.ORDER:
            self.copy(d).wait_send()


class Scatter:
    def __init__(self, at, part, got, ssem, rsem, start=0, size=None):
        self.at, self.part, self.got, self.ssem, self.rsem = at, part, got, ssem, rsem
        self.start, self.size = start, part.shape[1] if size is None else size
        self.blocks = pl.ds(self.start, self.size)
        p = at.piece
        self.plan = (
            (p(2, 0), at.yp),
            (p(2, 1), at.ym),
            (p(1, 0), at.yp),
            (p(1, 1), at.yp),
            (p(3, 1), at.ym),
            (p(3, 0), at.ym),
            (p(0, 1), at.xp),
        )

    def copy(self, k):
        sent, dev = self.plan[k]
        return remote(
            self.part.at[sent, self.blocks], self.got.at[k, self.blocks], self.ssem.at[k], self.rsem.at[k], dev
        )

    def send(self, *ks):
        for k in ks:
            self.copy(k).start()

    def wait(self, *ks):
        for k in ks:
            self.copy(k).wait_recv()

    def add(self, piece, *ks):
        def body(i, _):
            total = self.part[piece, i].astype(F32)
            for k in ks:
                total += self.got[k, i].astype(F32)
            self.part[piece, i] = total.astype(BF16)
            return 0

        lax.fori_loop(self.start, self.start + self.size, body, 0)

    def first(self):
        self.send(0, 1, 3, 5)

    def second(self):
        self.wait(1)
        self.add(self.plan[4][0], 1)
        self.send(4)
        self.wait(0)
        self.add(self.plan[2][0], 0)
        self.send(2)

    def third(self):
        self.wait(3, 4)
        self.add(self.plan[6][0], 3, 4)
        self.send(6)

    def last(self, out):
        self.wait(2, 5, 6)
        mine = self.at.piece(0, 0)

        def body(i, _):
            total = self.part[mine, i].astype(F32)
            for k in (2, 5, 6):
                total += self.got[k, i].astype(F32)
            out[i] = total
            return 0

        lax.fori_loop(self.start, self.start + self.size, body, 0)

    def drain(self):
        for k in range(7):
            self.copy(k).wait_send()


def kernel(
    v_hbm, g_hbm, c_hbm, f1_hbm, f2_hbm,
    dv_hbm, dg_hbm, o1_hbm, o2_hbm,
    val, gate, up, f1, f2_own, f2_a, f2_b, f2_near, gated, back, sendb, ret, mix, mov, movt,
    part1, got1, part2n, got2n, part2c, got2c, part2d, got2d, out1, out2n, out2c, out2d, out2,
    lsem, osem, g2as, g2ar, g2bs, g2br, g2ns, g2nr, g1as, g1ar, g1bs, g1br,
    s1as, s1ar, s1bs, s1br, s2ns, s2nr, s2cs, s2cr, s2ds, s2dr, bs, br, ms, mr,
):
    at = Place()
    a, h = at.a, at.h
    z, xh, core = a // 4, (a // 2) % 2, a % 2
    pair0 = a // 2

    loads = []

    def load(src, dst):
        cp = pltpu.make_async_copy(src, dst, lsem.at[len(loads)])
        cp.start()
        loads.append(cp)
        return cp

    f2_in = load(f2_hbm, f2_own)
    f1_in = load(f1_hbm, f1.at[h])
    rest = []
    for s in range(2):
        lanes = pl.ds(128 * s, 128)
        rest.append(load(c_hbm.at[s], up.at[:, lanes]))
        rest.append(load(v_hbm.at[s], val.at[:, lanes]))
        rest.append(load(g_hbm.at[s], gate.at[:, lanes]))

    barrier = pltpu.get_barrier_semaphore()

    def greet(k, _):
        pl.semaphore_signal(barrier, inc=1, device_id=(lax.rem(a + k, N_CTX), h), device_id_type=MESH)
        return 0

    for d in range(1, N_CH):
        pl.semaphore_signal(barrier, inc=1, device_id=(a, at.piece(d // 2, d % 2)), device_id_type=MESH)
    lax.fori_loop(1, N_CTX, greet, 0)
    far_a = Direct(at, f2_a, None, g2as, g2ar)
    far_b = Direct(at, f2_b, None, g2bs, g2br)
    near = Gather(at, f2_near, g2ns, g2nr)
    one_a = Gather(at, f1, g1as, g1ar, 0, 4)
    one_b = Gather(at, f1, g1bs, g1br, 4, 4)

    f2_in.wait()
    turn = lax.rem(256 - 32 * lax.rem(z + 3, 8), 256)

    def turn_block(k, _):
        x = pltpu.roll(f2_own[2 * k].astype(F32), turn, 1)
        y = pltpu.roll(f2_own[2 * k + 1].astype(F32), turn, 1)
        f2_a[h, k] = jnp.concatenate([x[:, :64], y[:, :64]], axis=1).astype(BF16)
        f2_b[h, k] = jnp.concatenate([x[:, 64:128], y[:, 64:128]], axis=1).astype(BF16)
        f2_near[h, 2 * k] = x[:, 128:].astype(BF16)
        f2_near[h, 2 * k + 1] = y[:, 128:].astype(BF16)
        return 0

    lax.fori_loop(0, 8, turn_block, 0)
    pl.semaphore_wait(barrier, N_CTX - 1 + N_CH - 1)
    far_a.send()
    far_b.send()
    for cp in rest:
        cp.wait()

    def multiply(k, _):
        rows = pl.ds(pl.multiple_of(k * 512, 512), 512)
        gated[k] = (val[rows, :].astype(F32) * gate[rows, :].astype(F32)).astype(BF16)
        return 0

    lax.fori_loop(0, 8, multiply, 0)

    r = lax.broadcasted_iota(jnp.int32, (256, 256), 0)
    c = lax.broadcasted_iota(jnp.int32, (256, 256), 1)
    swap = jnp.where(((r >> 4) == (c & 15)) & ((r & 15) == (c >> 4)), 1.0, 0.0).astype(BF16)

    def back_copy(dst, src):
        row = lax.rem(src // 4 - dst // 4 + 14, 8) * 64 + lax.rem(src, 4) * 16
        return remote(sendb.at[dst], ret.at[:, pl.ds(pl.multiple_of(row, 16), 16), :], bs.at[dst], br.at[src], (dst, h))

    def upstream(k):
        return up[pl.ds(pl.multiple_of(k * 256, 256), 256), :]

    def back_send(first, row0, count):
        def send(k, _):
            xt = lax.rem(xh + k, 2)
            p = lax.rem(z + first + k // 2, 8) * 2 + xt
            row = pl.multiple_of(row0 + (k // 2) * 32 + xt * 16, 16)
            x = back[:, pl.ds(row, 16), :].reshape(256, 256)
            t = dot(swap, x, ((1,), (0,))).astype(BF16).reshape(2, 8, 16, 256)
            sendb[2 * p] = t[0]
            sendb[2 * p + 1] = t[1]

            @pl.when(p != pair0)
            def _():
                back_copy(2 * p + core, a).start()

            back_copy(2 * p + 1 - core, a).start()
            return 0

        lax.fori_loop(0, count, send, 0, unroll=2)

    def back_quarter(w_ref, first, row0):
        def block(k, _):
            w = w_ref[:, k].reshape(256, 128)
            back[2 * k, row0:row0 + 64] = dot(w[:, :64], upstream(2 * k), ((0,), (0,))).astype(BF16)
            back[2 * k + 1, row0:row0 + 64] = dot(w[:, 64:], upstream(2 * k + 1), ((0,), (0,))).astype(BF16)
            return 0

        lax.fori_loop(0, 8, block, 0, unroll=2)
        back_send(first, row0, 4)

    def back_near(k, _):
        back[k, 128:] = dot(f2_near[:, k].reshape(256, 128), upstream(k), ((0,), (0,))).astype(BF16)
        return 0

    far_a.wait()
    near.send(0, 1, 2)
    f1_in.wait()
    one_a.send(0, 1, 2)
    back_quarter(f2_a, 3, 0)
    far_b.wait()
    back_quarter(f2_b, 5, 64)
    near.wait(0)
    near.send(3, 4)
    one_a.wait(0)
    one_a.send(3, 4)
    near.wait(1)
    near.send(5)
    one_b.send(0, 1, 2)
    near.wait(4)
    near.send(6)
    one_a.wait(1)
    one_a.send(5)
    one_b.wait(0)
    one_b.send(3, 4)
    one_a.wait(4)
    one_a.send(6)
    one_b.wait(1)
    one_b.send(5)
    near.wait(2, 3, 5, 6)
    lax.fori_loop(0, 16, back_near, 0, unroll=4)
    back_send(7, 128, 8)
    ret[:, pl.ds(pl.multiple_of(384 + lax.rem(a, 4) * 16, 16), 16), :] = sendb[a]
    one_b.wait(4)
    one_b.send(6)

    def mix_block(i, _):
        mix[i] = dot(f1[:, i].reshape(512, 512), gated[i], ((1,), (0,))).astype(BF16)
        return 0

    def mix_copy(c, dst, slot):
        rows = pl.ds(pl.multiple_of(16 * dst, 16), 16)
        blocks = pl.ds(4 * c, 4)
        return remote(mix.at[blocks, rows, :], mov.at[slot, blocks], ms.at[c, dst], mr.at[c, slot], (dst, h))

    def mix_send(c, first, count):
        def send(k, _):
            p = lax.rem(z + first + k // 2, 8) * 2 + lax.rem(xh + k, 2)

            @pl.when(p != pair0)
            def _():
                mix_copy(c, 2 * p + core, a).start()

            mix_copy(c, 2 * p + 1 - core, a).start()
            return 0

        lax.fori_loop(0, count, send, 0)

    one_a.wait(2, 3, 5, 6)
    lax.fori_loop(0, 4, mix_block, 0, unroll=2)
    mix_send(0, 6, 12)

    def back_wait(k, _):
        src = lax.rem(a + k, N_CTX)
        back_copy(a, src).wait_recv()
        return 0

    lax.fori_loop(1, N_CTX, back_wait, 0)

    def grad_one_block(i, _):
        t = dot(ret[i], gated[i], ((1,), (1,))).astype(BF16).reshape(8, 64, 512)
        for q in range(8):
            part1[lax.rem(z + 2 + q, 8), i] = t[q]
        return 0

    def grad_input_block(i, _):
        w = jnp.concatenate([f1[lax.rem(z + 2 + q, 8), i] for q in range(8)], axis=0)
        grad = dot(w, ret[i], ((0,), (0,)))
        rows = pl.ds(pl.multiple_of(i * 512, 512), 512)
        v, g = val[rows, :].astype(F32), gate[rows, :].astype(F32)
        val[rows, :] = (grad * g).astype(BF16)
        gate[rows, :] = (grad * v).astype(BF16)
        return 0

    rs1a = Scatter(at, part1, got1, s1as, s1ar, 0, 4)
    rs1b = Scatter(at, part1, got1, s1bs, s1br, 4, 4)
    lax.fori_loop(0, 4, grad_one_block, 0, unroll=2)
    rs1a.first()
    one_b.wait(2, 3, 5, 6)
    lax.fori_loop(4, 8, mix_block, 0, unroll=2)
    mix_send(1, 6, 12)
    mov[a] = mix[:, pl.ds(pl.multiple_of(16 * a, 16), 16), :]
    lax.fori_loop(4, 8, grad_one_block, 0, unroll=2)
    rs1b.first()
    lax.fori_loop(0, 8, grad_input_block, 0, unroll=2)
    mix_send(0, 4, 4)
    mix_send(1, 4, 4)
    rs1a.second()
    stores = []

    def store(src, dst):
        cp = pltpu.make_async_copy(src, dst, osem.at[len(stores)])
        cp.start()
        stores.append(cp)

    for s in range(2):
        lanes = pl.ds(128 * s, 128)
        store(val.at[:, lanes], dv_hbm.at[s])
        store(gate.at[:, lanes], dg_hbm.at[s])

    def take(last, row0, count):
        def body(k, _):
            xt = lax.rem(xh + k, 2)
            p = lax.rem(z + last + 8 - k // 2, 8) * 2 + xt

            @pl.when(p != pair0)
            def _():
                mix_copy(0, 2 * p + core, 2 * p + core).wait_recv()
                mix_copy(1, 2 * p + core, 2 * p + core).wait_recv()

            mix_copy(0, 2 * p + 1 - core, 2 * p + 1 - core).wait_recv()
            mix_copy(1, 2 * p + 1 - core, 2 * p + 1 - core).wait_recv()
            x = mov[pl.ds(2 * p, 2)].reshape(256, 256)
            t = dot(swap, x, ((1,), (0,))).astype(BF16).reshape(16, 16, 256)
            row = pl.multiple_of(row0 - (k // 2) * 32 + xt * 16, 16)
            movt[:, pl.ds(row, 16), :] = t
            return 0

        lax.fori_loop(0, count, body, 0, unroll=2)

    def grad_two_near(k, _):
        t = dot(upstream(k), movt[k, 128:], ((1,), (1,))).astype(BF16)
        part2n[:, k] = t.reshape(8, 32, 128)
        return 0

    def grad_two_quarter(part, row0):
        def body(k, _):
            t = [dot(upstream(2 * k + e), movt[2 * k + e, row0:row0 + 64], ((1,), (1,))) for e in range(2)]
            part[:, k] = jnp.concatenate(t, axis=1).astype(BF16).reshape(8, 32, 128)
            return 0

        lax.fori_loop(0, 8, body, 0, unroll=2)

    rs2n = Scatter(at, part2n, got2n, s2ns, s2nr)
    rs2c = Scatter(at, part2c, got2c, s2cs, s2cr)
    rs2d = Direct(at, part2d, got2d, s2ds, s2dr)
    take(10, 224, 8)
    lax.fori_loop(0, 16, grad_two_near, 0, unroll=4)
    rs2n.first()
    rs1a.third()
    take(6, 96, 4)
    grad_two_quarter(part2c, 64)
    rs2c.first()
    rs1b.second()
    rs2n.second()
    rs2c.second()
    rs1b.third()
    take(4, 32, 4)
    grad_two_quarter(part2d, 0)
    rs2d.send()
    rs2n.third()
    rs2c.third()
    rs1a.last(out1)
    rs1b.last(out1)
    store(out1, o1_hbm)
    rs2n.last(out2n)
    rs2c.last(out2c)
    rs2d.last(out2d)
    unturn = 32 * lax.rem(z + 3, 8)

    def unturn_block(k, _):
        for e in range(2):
            lanes = slice(64 * e, 64 * e + 64)
            x = jnp.concatenate([out2d[k, :, lanes], out2c[k, :, lanes], out2n[2 * k + e]], axis=1)
            out2[2 * k + e] = pltpu.roll(x, unturn, 1)
        return 0

    lax.fori_loop(0, 8, unturn_block, 0)
    store(out2, o2_hbm)

    def drain(k, _):
        dst = lax.rem(a + k, N_CTX)
        back_copy(dst, a).wait_send()
        mix_copy(0, dst, a).wait_send()
        mix_copy(1, dst, a).wait_send()
        return 0

    lax.fori_loop(1, N_CTX, drain, 0)
    for x in (far_a, far_b, near, one_a, one_b, rs1a, rs1b, rs2n, rs2c, rs2d):
        x.drain()
    for cp in stores:
        cp.wait()


def per_device(values, gate, cotangent, factor_one, factor_two):
    vm = pltpu.VMEM
    dma = pltpu.SemaphoreType.DMA
    shapes = (
        jax.ShapeDtypeStruct(values.shape, BF16),
        jax.ShapeDtypeStruct(values.shape, BF16),
        jax.ShapeDtypeStruct(factor_one.shape, F32),
        jax.ShapeDtypeStruct(factor_two.shape, F32),
    )
    scratch = [
        vm((4096, 256), BF16), vm((4096, 256), BF16), vm((4096, 256), BF16),
        vm((8, 8, 64, 512), BF16),
        vm((16, 32, 256), BF16), vm((8, 8, 32, 128), BF16), vm((8, 8, 32, 128), BF16), vm((8, 16, 32, 128), BF16),
        vm((8, 512, 256), BF16),
        vm((16, 256, 256), BF16),
        vm((32, 8, 16, 256), BF16),
        vm((8, 512, 256), BF16),
        vm((8, 512, 256), BF16),
        vm((32, 8, 16, 256), BF16),
        vm((16, 256, 256), BF16),
        vm((8, 8, 64, 512), BF16), vm((7, 8, 64, 512), BF16),
        vm((8, 16, 32, 128), BF16), vm((7, 16, 32, 128), BF16),
        vm((8, 8, 32, 128), BF16), vm((7, 8, 32, 128), BF16),
        vm((8, 8, 32, 128), BF16), vm((7, 8, 32, 128), BF16),
        vm((8, 64, 512), F32),
        vm((16, 32, 128), F32), vm((8, 32, 128), F32), vm((8, 32, 128), F32), vm((16, 32, 256), F32),
        dma((8,)), dma((6,)),
        *[dma((7,)) for _ in range(20)],
        dma((32,)), dma((32,)), dma((2, 32)), dma((2, 32)),
    ]
    anywhere = pl.BlockSpec(memory_space=pl.ANY)
    return pl.pallas_call(
        kernel,
        out_shape=shapes,
        in_specs=[anywhere] * 5,
        out_specs=(anywhere,) * 4,
        scratch_shapes=scratch,
        compiler_params=pltpu.CompilerParams(
            collective_id=0, has_side_effects=True, vmem_limit_bytes=46 * 1024 * 1024
        ),
        name="monarch_backward",
    )(values, gate, cotangent, factor_one, factor_two)


def solution(mesh):
    tokens = P(None, "ctx", "ch")
    rows = P("ctx", "ch", None)
    return jax.shard_map(
        per_device,
        mesh=mesh,
        in_specs=(tokens, tokens, tokens, rows, rows),
        out_specs=(tokens, tokens, rows, rows),
        check_vma=False,
    )
```

time: 160 us -> 158 us (0.988)
    unnamed x10 -> x8, local copies, waits for them, and re-layouts: 7.34 us -> 6.39 us
where the time goes in v3:
time: 158 us; the launch traced here: 157 us
  Pallas kernels  150 us (95%)
  local copies, waits for them, and re-layouts  6.39 us (4%)
    pallas_call x1, Pallas kernels, per_device(): pl.pallas_call(kernel, out_shape=shapes, in_specs=[anywhere] * 5, out_spe...  150 us
    unnamed x8, local copies, waits for them, and re-layouts  6.39 us

profile of v3, /device:TPU:42, one launch (start us, length us, event | category | flops | bytes accessed | tf_op | source)
XLA Modules:
  0.0 156.9 jit_solution(5011192428853420341)
XLA Ops:
  0.6 0.0 copy-start
  0.6 1.0 copy-done
  1.7 0.0 copy-start.1
  1.7 0.9 copy-done.1
  2.6 149.9 %monarch_backward.1 = (bf16[2,4096,128]{2,1,0:T(8,128)(2,1)S(1)}, bf16[2,4096,128]{2,1,0:T(8,128)(2,1)S(1)}, f32[8,64,512]{2,1,0:T(8,128)S(1)}, f32[16,32,256]{2,1,0:T(8,128)S(1)}) custom-call(bf16[2,4096,128]{2,1,0:T(8,128)(2,1)} %v_hbm.1, bf16[2,4096,128]{2,1,0:T(8,128)(2,1)} %g_hbm.1, bf16[2,4096,128]{2,1,0:T(8,128)(2,1)} %c_hbm.1, ...), custom_call_target="tpu_custom_call" | custom-call | tf_op jit(solution)/shard_map/monarch_backward/pallas_call | solution.py:531
  152.5 1.3 copy.13
  153.8 1.3 copy.14
  155.2 1.0 copy.15
  156.1 0.8 copy.16
Async XLA Ops:
  0.6 1.0 copy-start
  1.7 0.9 copy-start.1

commit v4 on v3

--- a/solution.py
+++ b/solution.py
@@ -253,7 +253,6 @@
     lax.fori_loop(0, 8, turn_block, 0)
     pl.semaphore_wait(barrier, N_CTX - 1 + N_CH - 1)
     far_a.send()
-    far_b.send()
     for cp in rest:
         cp.wait()
 
@@ -263,6 +262,7 @@
         return 0
 
     lax.fori_loop(0, 8, multiply, 0)
+    far_b.send()
 
     r = lax.broadcasted_iota(jnp.int32, (256, 256), 0)
     c = lax.broadcasted_iota(jnp.int32, (256, 256), 1)
@@ -459,10 +459,10 @@
     rs1b.second()
     rs2n.second()
     rs2c.second()
-    rs1b.third()
     take(4, 32, 4)
     grad_two_quarter(part2d, 0)
     rs2d.send()
+    rs1b.third()
     rs2n.third()
     rs2c.third()
     rs1a.last(out1)

time: 158 us -> 154 us (0.975)
  Pallas kernels: 150 us -> 147 us
    pallas_call x1, Pallas kernels: 150 us -> 147 us  [per_device(): pl.pallas_call(kernel, out_shape=shapes, in_specs=[anywhere] * 5, out_spe...]
where the time goes in v4:
time: 154 us
  Pallas kernels  147 us (95%)
  local copies, waits for them, and re-layouts  6.39 us (4%)
    pallas_call x1, Pallas kernels, per_device(): pl.pallas_call(kernel, out_shape=shapes, in_specs=[anywhere] * 5, out_spe...  147 us
    unnamed x8, local copies, waits for them, and re-layouts  6.39 us

profile of v4, /device:TPU:42, one launch (start us, length us, event | category | flops | bytes accessed | tf_op | source)
XLA Modules:
  0.0 154.3 jit_solution(38504265309357052)
XLA Ops:
  0.6 0.0 copy-start
  0.6 1.0 copy-done
  1.7 0.0 copy-start.1
  1.7 0.9 copy-done.1
  2.6 147.2 %monarch_backward.1 = (bf16[2,4096,128]{2,1,0:T(8,128)(2,1)S(1)}, bf16[2,4096,128]{2,1,0:T(8,128)(2,1)S(1)}, f32[8,64,512]{2,1,0:T(8,128)S(1)}, f32[16,32,256]{2,1,0:T(8,128)S(1)}) custom-call(bf16[2,4096,128]{2,1,0:T(8,128)(2,1)} %v_hbm.1, bf16[2,4096,128]{2,1,0:T(8,128)(2,1)} %g_hbm.1, bf16[2,4096,128]{2,1,0:T(8,128)(2,1)} %c_hbm.1, ...), custom_call_target="tpu_custom_call" | custom-call | tf_op jit(solution)/shard_map/monarch_backward/pallas_call | solution.py:531
  149.9 1.3 copy.13
  151.2 1.3 copy.14
  152.5 1.0 copy.15
  153.5 0.8 copy.16
Async XLA Ops:
  0.6 1.0 copy-start
  1.7 0.9 copy-start.1

commit v5 on v4

--- a/solution.py
+++ b/solution.py
@@ -112,7 +112,7 @@
             out[i] = total
             return 0
 
-        lax.fori_loop(0, self.part.shape[1], body, 0)
+        lax.fori_loop(0, self.part.shape[1], body, 0, unroll=4)
 
     def drain(self):
         for d in self.ORDER:
@@ -157,7 +157,7 @@
             self.part[piece, i] = total.astype(BF16)
             return 0
 
-        lax.fori_loop(self.start, self.start + self.size, body, 0)
+        lax.fori_loop(self.start, self.start + self.size, body, 0, unroll=4)
 
     def first(self):
         self.send(0, 1, 3, 5)
@@ -186,7 +186,7 @@
             out[i] = total
             return 0
 
-        lax.fori_loop(self.start, self.start + self.size, body, 0)
+        lax.fori_loop(self.start, self.start + self.size, body, 0, unroll=4)
 
     def drain(self):
         for k in range(7):
@@ -250,7 +250,7 @@
         f2_near[h, 2 * k + 1] = y[:, 128:].astype(BF16)
         return 0
 
-    lax.fori_loop(0, 8, turn_block, 0)
+    lax.fori_loop(0, 8, turn_block, 0, unroll=4)
     pl.semaphore_wait(barrier, N_CTX - 1 + N_CH - 1)
     far_a.send()
     for cp in rest:
@@ -480,7 +480,7 @@
             out2[2 * k + e] = pltpu.roll(x, unturn, 1)
         return 0
 
-    lax.fori_loop(0, 8, unturn_block, 0)
+    lax.fori_loop(0, 8, unturn_block, 0, unroll=4)
     store(out2, o2_hbm)
 
     def drain(k, _):

time: 154 us -> 153 us (level)
  no operation moved by 1% of the time
where the time goes in v5:
time: 153 us
  Pallas kernels  146 us (95%)
  local copies, waits for them, and re-layouts  6.39 us (4%)
    pallas_call x1, Pallas kernels, per_device(): pl.pallas_call(kernel, out_shape=shapes, in_specs=[anywhere] * 5, out_spe...  146 us
    unnamed x8, local copies, waits for them, and re-layouts  6.39 us

profile of v5, /device:TPU:42, one launch (start us, length us, event | category | flops | bytes accessed | tf_op | source)
XLA Modules:
  0.0 153.3 jit_solution(9534416787326421926)
XLA Ops:
  0.6 0.0 copy-start
  0.6 1.0 copy-done
  1.7 0.0 copy-start.1
  1.7 0.9 copy-done.1
  2.6 146.3 %monarch_backward.1 = (bf16[2,4096,128]{2,1,0:T(8,128)(2,1)S(1)}, bf16[2,4096,128]{2,1,0:T(8,128)(2,1)S(1)}, f32[8,64,512]{2,1,0:T(8,128)S(1)}, f32[16,32,256]{2,1,0:T(8,128)S(1)}) custom-call(bf16[2,4096,128]{2,1,0:T(8,128)(2,1)} %v_hbm.1, bf16[2,4096,128]{2,1,0:T(8,128)(2,1)} %g_hbm.1, bf16[2,4096,128]{2,1,0:T(8,128)(2,1)} %c_hbm.1, ...), custom_call_target="tpu_custom_call" | custom-call | tf_op jit(solution)/shard_map/monarch_backward/pallas_call | solution.py:531
  148.9 1.3 copy.13
  150.2 1.3 copy.14
  151.5 1.0 copy.15
  152.5 0.8 copy.16
Async XLA Ops:
  0.6 1.0 copy-start
  1.7 0.9 copy-start.1
